TPU v7x, 128 devices: a whole 4x4x4 slice. The times are simulated.
128 devices in a mesh: side: 2 (over y_lo), owner: 32 (over z, x, y_hi), seq: 2 (over core).
Axes of the slice: x: 4, y: 4 (y_hi: 2, y_lo: 2; y = y_hi * 2 + y_lo), z: 4, core: 2. Of those that a mesh axis runs over, the one named last changes fastest.
Arguments:
- prompt_hidden: bfloat16 [16384, 7168], P(('side', 'seq'), 'owner'), may hold values from -12 to 12
- latent_weight: bfloat16 [7168, 576], P('owner'), may hold values from -2 to 2
- kv_gain: float32 [512], replicated, may hold values from 0.25 to 1.75
- prompt_lengths: int32 [4], replicated, may hold values from 1 to 8192, 16384 in all
- destination: int32 [16384, 1], P(('side', 'seq')), may hold values from 0 to 127; in each aligned block of 128 rows (0 to 127, 128 to 255, ...) at most 2 rows name the same one
- request_order: int32 [128], replicated, may hold values from 0 to 127, each once
- cache: bfloat16 [128, 16384, 576], P('owner', ('side', 'seq')), may hold values from -8 to 8
- cache_lengths: int32 [128], P('owner'), may hold values from 2048 to 16384, as said below
- queries: bfloat16 [4, 128, 128, 576], P(None, 'owner'), may hold values from -32 to 32
- new_rows: bfloat16 [4, 128, 576], P(None, 'owner'), may hold values from -4 to 4
Outputs:
- attention: bfloat16 [4, 128, 128, 512], P(None, 'owner', ('side', 'seq'))
Inputs may be any that keep to these rules, and one draw needn't show every extreme that they name: `destination`: within each aligned block of 128 rows no request is named by more than 2 rows, a bound that some block reaches. `request_order`: each request once. `cache_lengths`: some slot has exactly 16384 live positions. `prompt_lengths`: the prompts lie in order in the block and their lengths sum to 16384.
All inputs are finite; a program needn't handle non-finite values.
Results may differ from a plain program's by a relative error of at most 0.012.
Values may be sent and summed in bfloat16 or wider, within the bound.
A program may use at most 192 MiB of HBM per device.

v0:
```python
import jax
import jax.numpy as jnp
from jax import lax
from jax.sharding import PartitionSpec as P

softmax_scale = 192.0 ** (-0.5)
rope_theta = 10000.0
norm_eps = 1e-06
masked_score = -1e30


def joined(x, axis, combine):
    everything = jax.tree.map(lambda part: lax.all_gather(part, axis), x)
    first = jax.tree.map(lambda part: part[0], everything)

    def lap(k, so_far):
        return combine(so_far, jax.tree.map(lambda part: part[k], everything))

    return lax.fori_loop(1, lax.axis_size(axis), lap, first)


def rotate_pairs(rope_part, positions):
    half_width = rope_part.shape[1] // 2
    frequency = rope_theta ** (-jnp.arange(half_width, dtype=jnp.float32) / half_width)
    angles = positions.astype(jnp.float32)[:, None] * frequency[None, :]
    cosine = jnp.cos(angles)
    sine = jnp.sin(angles)
    first_half = rope_part[:, :half_width]
    second_half = rope_part[:, half_width:]
    return jnp.concatenate(
        [first_half * cosine - second_half * sine, first_half * sine + second_half * cosine], axis=1
    )


def latent_rows(projected, kv_gain, positions):
    latent_width = kv_gain.shape[0]
    latent = projected[:, :latent_width]
    mean_square = jnp.mean(latent * latent, axis=1, keepdims=True)
    normed = latent * lax.rsqrt(mean_square + norm_eps) * kv_gain[None, :]
    return jnp.concatenate(
        [normed, rotate_pairs(projected[:, latent_width:], positions)], axis=1
    ).astype(jnp.bfloat16)


def token_positions(tokens, prompt_lengths):
    starts = jnp.cumsum(prompt_lengths) - prompt_lengths
    began = jnp.where(starts[None, :] <= tokens[:, None], starts[None, :], 0)
    return tokens - jnp.max(began, axis=1)


def bucket_places(dest_blocks, request_order, req_dev, bound_rows):
    slot_ids = jnp.arange(request_order.shape[0], dtype=jnp.int32)
    matches = request_order[None, None, :] == dest_blocks[:, :, None]
    slots = jnp.sum(jnp.where(matches, slot_ids[None, None, :], 0), axis=2)
    row_ids = jnp.arange(dest_blocks.shape[1], dtype=jnp.int32)
    earlier = (dest_blocks[:, :, None] == dest_blocks[:, None, :]) & (
        row_ids[None, None, :] < row_ids[None, :, None]
    )
    ranking = jnp.sum(earlier.astype(jnp.int32), axis=2)
    return (slots // req_dev, slots % req_dev * bound_rows + ranking)


def join_partials(first_part, second_part):
    top_score = jnp.maximum(first_part[0], second_part[0])
    first_scale = jnp.exp(first_part[0] - top_score)
    second_scale = jnp.exp(second_part[0] - top_score)
    return (
        top_score,
        first_part[1] * first_scale + second_part[1] * second_scale,
        first_part[2] * first_scale[..., None] + second_part[2] * second_scale[..., None],
    )


def on_device(
    prompt_hidden,
    latent_weight,
    kv_gain,
    prompt_lengths,
    destination,
    request_order,
    cache,
    cache_lengths,
    queries,
    new_rows,
):
    owners = lax.axis_size("owner")
    owner_rank = lax.axis_index("owner")
    quarters = lax.axis_size("side") * lax.axis_size("seq")
    quarter = lax.axis_index("side") * lax.axis_size("seq") + lax.axis_index("seq")
    quarter_rows = prompt_hidden.shape[0]
    block_rows = quarter_rows // owners
    req_dev = cache.shape[0]
    bound_rows = max(2, 2 * block_rows // (req_dev * owners))
    capacity = req_dev * bound_rows
    key_width = latent_weight.shape[1]
    latent_width = kv_gain.shape[0]
    projected = lax.psum_scatter(
        jnp.dot(prompt_hidden, latent_weight, preferred_element_type=jnp.float32).astype(
            jnp.bfloat16
        ),
        "owner",
        scatter_dimension=0,
        tiled=True,
    ).astype(jnp.float32)
    tokens = (
        quarter * quarter_rows + owner_rank * block_rows + jnp.arange(block_rows, dtype=jnp.int32)
    )
    handed = latent_rows(projected, kv_gain, token_positions(tokens, prompt_lengths))
    own_dest = lax.dynamic_slice_in_dim(destination[:, 0], owner_rank * block_rows, block_rows, 0)
    target, position = bucket_places(own_dest[None, :], request_order, req_dev, bound_rows)
    outgoing = (
        jnp.zeros((owners, capacity, key_width), jnp.bfloat16)
        .at[target[0], position[0]]
        .set(handed)
    )
    marks = jnp.zeros((owners, capacity), jnp.int32).at[target[0], position[0]].set(1)
    received, filled = (
        lax.all_to_all(outgoing, "owner", split_axis=0, concat_axis=0, tiled=True),
        lax.all_to_all(marks, "owner", split_axis=0, concat_axis=0, tiled=True),
    )
    cache_rows = cache.shape[1]
    positions_cache = quarter * cache_rows + jnp.arange(cache_rows, dtype=jnp.int32)
    handed_keys = received.reshape(owners, req_dev, bound_rows, key_width)
    handed_live = filled.reshape(owners, req_dev, bound_rows) > 0
    maxima = []
    totals = []
    weighted = []
    for request in range(req_dev):
        query_rows = queries[:, request]
        cache_keys = cache[request]
        own_keys = handed_keys[:, request].reshape(owners * bound_rows, key_width)
        live_own = handed_live[:, request].reshape(owners * bound_rows)[None, None, :]
        live_cache = (positions_cache < cache_lengths[request])[None, None, :]
        scores_cache = (
            jnp.einsum("shk,ck->shc", query_rows, cache_keys, preferred_element_type=jnp.float32)
            * softmax_scale
        )
        scores_own = (
            jnp.einsum("shk,ck->shc", query_rows, own_keys, preferred_element_type=jnp.float32)
            * softmax_scale
        )
        top_score = jnp.maximum(
            jnp.max(jnp.where(live_cache, scores_cache, masked_score), axis=2),
            jnp.max(jnp.where(live_own, scores_own, masked_score), axis=2),
        )
        weights_cache = jnp.where(live_cache, jnp.exp(scores_cache - top_score[:, :, None]), 0.0)
        weights_own = jnp.where(live_own, jnp.exp(scores_own - top_score[:, :, None]), 0.0)
        totals.append(jnp.sum(weights_cache, axis=2) + jnp.sum(weights_own, axis=2))
        summed = jnp.einsum(
            "shc,cl->shl",
            weights_cache.astype(jnp.bfloat16),
            cache_keys[:, :latent_width],
            preferred_element_type=jnp.float32,
        )
        summed = summed + jnp.einsum(
            "shc,cl->shl",
            weights_own.astype(jnp.bfloat16),
            own_keys[:, :latent_width],
            preferred_element_type=jnp.float32,
        )
        weighted.append(summed)
        maxima.append(top_score)
    partial_max = jnp.stack(maxima, axis=1)
    partial_total = jnp.stack(totals, axis=1)
    partial_sum = jnp.stack(weighted, axis=1)
    own_heads = queries.shape[2] // quarters
    combined = joined((partial_max, partial_total, partial_sum), ("side", "seq"), join_partials)
    merged = tuple(
        (lax.dynamic_slice_in_dim(member, quarter * own_heads, own_heads, 2) for member in combined)
    )
    own_queries = lax.dynamic_slice_in_dim(queries, quarter * own_heads, own_heads, 2)
    step_count = queries.shape[0]
    step_order = jnp.arange(step_count, dtype=jnp.int32)
    live_new = (step_order[None, :] <= step_order[:, None])[:, None, None, :]
    scores_new = (
        jnp.einsum("srhk,trk->srht", own_queries, new_rows, preferred_element_type=jnp.float32)
        * softmax_scale
    )
    top_score = jnp.maximum(
        merged[0], jnp.max(jnp.where(live_new, scores_new, masked_score), axis=3)
    )
    weights_new = jnp.where(live_new, jnp.exp(scores_new - top_score[..., None]), 0.0)
    rescale = jnp.exp(merged[0] - top_score)
    denominator = merged[1] * rescale + jnp.sum(weights_new, axis=3)
    accumulated = merged[2] * rescale[..., None] + jnp.einsum(
        "srht,trl->srhl",
        weights_new.astype(jnp.bfloat16),
        new_rows[:, :, :latent_width],
        preferred_element_type=jnp.float32,
    )
    return (accumulated / denominator[..., None]).astype(jnp.bfloat16)


def solution(mesh):
    return jax.shard_map(
        on_device,
        mesh=mesh,
        in_specs=(
            P(("side", "seq"), "owner"),
            P("owner", None),
            P(),
            P(),
            P(("side", "seq"), None),
            P(),
            P("owner", ("side", "seq"), None),
            P("owner"),
            P(None, "owner", None, None),
            P(None, "owner", None),
        ),
        out_specs=P(None, "owner", ("side", "seq"), None),
        check_vma=False,
    )
```

profile of v0, /device:TPU:1, one launch (start us, length us, event | category | flops | bytes accessed | tf_op | source)
XLA Modules:
  0.0 459.5 jit_solution(5928857363585149990)
XLA Ops:
  8.0 4.6 convolution_convert_fusion
  12.6 7.6 %copy.160 = bf16[4096,576]{1,0:T(8,128)(2,1)} copy(bf16[4096,576]{0,1:T(8,128)(2,1)} %convolution_convert_fusion) | data formatting | bytes 9437184
  21.2 6.4 %scatter_fusion = s32[32,8]{0,1:T(8,128)S(1)} fusion(s32[32,8]{0,1:T(8,128)S(1)} %broadcast_in_dim.198, s32[128]{0:T(128)S(1)} %fusion.115, s32[128]{0:T(128)S(1)} %broadcast.404), kind=kCustom, calls=%fused_computation | custom fusion | bytes 2560 | tf_op jit(solution)/shard_map/scatter | solution.py:116
  28.3 11.5 %all-to-all-start = ((s32[32,1,8]{2,1,0:T(1,128)}), s32[32,1,8]{2,1,0:T(1,128)S(1)}, u32[]{:S(2)}, u32[]{:S(2)}) async-start(s32[32,1,8]{2,1,0:T(1,128)} %copy.120), calls=%async_computation | async-start | bytes 32768 | tf_op jit(solution)/shard_map/all_to_all | solution.py:119
  43.4 9.7 %select_reduce_fusion = (f32[4,128]{1,0:T(4,128)S(1)}, f32[4,128,4096]{2,1,0:T(8,128)}) fusion(pred[4096]{0:T(1024)(128)(4,1)S(1)} %get-tuple-element.279, bf16[4,4096,576]{1,2,0:T(8,128)(2,1)} %param.18, bf16[4,4,128,576]{2,3,1,0:T(8,128)(2,1)} %param.20), kind=kOutput, calls=%fused_computation.16 | convolution fusion | flops 2422210048 | bytes 13703168 | tf_op jit(solution)/shard_map/shk,ck->shc/dot_general | solution.py:135
  53.1 8.5 %select_reduce_fusion.1 = (f32[4,128]{1,0:T(4,128)S(1)}, f32[4,128,4096]{2,1,0:T(8,128)}) fusion(pred[4096]{0:T(1024)(128)(4,1)S(1)} %get-tuple-element.280, bf16[4,4096,576]{1,2,0:T(8,128)(2,1)} %param.18, bf16[4,4,128,576]{2,3,1,0:T(8,128)(2,1)S(1)} %copy-done.6), kind=kOutput, calls=%fused_computation.17 | convolution fusion | flops 2422210048 | bytes 13703168 | tf_op jit(solution)/shard_map/shk,ck->shc/dot_general | solution.py:135
  61.6 8.6 %select_reduce_fusion.2 = (f32[4,128]{1,0:T(4,128)S(1)}, f32[4,128,4096]{2,1,0:T(8,128)}) fusion(pred[4096]{0:T(1024)(128)(4,1)S(1)} %get-tuple-element.281, bf16[4,4096,576]{1,2,0:T(8,128)(2,1)} %param.18, bf16[4,4,128,576]{2,3,1,0:T(8,128)(2,1)S(1)} %copy-done.6), kind=kOutput, calls=%fused_computation.18 | convolution fusion | flops 2422210048 | bytes 13703168 | tf_op jit(solution)/shard_map/shk,ck->shc/dot_general | solution.py:135
  70.2 6.1 %select_reduce_fusion.3 = (f32[4,128]{1,0:T(4,128)S(1)}, f32[4,128,4096]{2,1,0:T(8,128)}) fusion(pred[4096]{0:T(1024)(128)(4,1)S(1)} %get-tuple-element.282, bf16[4,4096,576]{1,2,0:T(8,128)(2,1)S(1)} %bitcast.236, bf16[4,4,128,576]{2,3,1,0:T(8,128)(2,1)S(1)} %copy-done.6), kind=kOutput, calls=%fused_computation.19 | convolution fusion | flops 2422210048 | bytes 13703168 | tf_op jit(solution)/shard_map/shk,ck->shc/dot_general | solution.py:135
  76.3 6.6 %slice_bitcast_fusion.11 = (bf16[4096,576]{0,1:T(8,128)(2,1)}, bf16[4096,576]{0,1:T(8,128)(2,1)}, bf16[4096,576]{0,1:T(8,128)(2,1)}, bf16[4096,576]{0,1:T(8,128)(2,1)}) fusion(bf16[4,4096,576]{1,2,0:T(8,128)(2,1)S(1)} %bitcast.236), kind=kLoop, calls=%fused_computation.69 | loop fusion | bytes 37748736 | tf_op jit(solution)/shard_map/squeeze | solution.py:130
  83.0 113.6 %reduce-scatter.4.cloned.1.call-done = bf16[128,576]{1,0:T(8,128)(2,1)} async-done(((bf16[4096,576]{1,0:T(8,128)(2,1)}), bf16[128,576]{1,0:T(8,128)(2,1)}) %reduce-scatter.4.cloned.1.call-update) | async-done | bytes 147472
  199.0 17.3 %scatter_fusion.1 = bf16[32,8,576]{2,1,0:T(8,128)(2,1)} fusion(bf16[32,8,576]{2,1,0:T(8,128)(2,1)} %broadcast_in_dim.205, s32[128]{0:T(128)S(1)} %fusion.115, bf16[128,576]{1,0:T(8,128)(2,1)S(1)} %copy.123), kind=kCustom, calls=%fused_computation.1 | custom fusion | bytes 443392 | tf_op jit(solution)/shard_map/scatter | solution.py:114
  216.4 4.3 all-to-all-start.1
  221.9 8.9 %all-to-all-done.1 = bf16[32,8,576]{2,1,0:T(8,128)(2,1)S(1)} async-done(((bf16[32,8,576]{2,1,0:T(8,128)(2,1)}), bf16[32,8,576]{2,1,0:T(8,128)(2,1)S(1)}, u32[]{:S(2)}, u32[]{:S(2)}) %all-to-all-start.1) | async-done | bytes 294944 | tf_op jit(solution)/shard_map/all_to_all | solution.py:118
  237.4 7.1 %fusion.20 = f32[4,128,512]{2,1,0:T(8,128)S(1)} fusion(f32[4,128,4096]{2,1,0:T(8,128)} %get-tuple-element.262, bf16[4096,576]{0,1:T(8,128)(2,1)} %get-tuple-element.245, f32[4,128]{1,0:T(4,128)S(1)} %max.87, pred[4096]{0:T(1024)(128)(4,1)S(1)} %get-tuple-element.279), kind=kOutput, calls=%fused_computation.37 | convolution fusion | flops 2155872256 | bytes 13637632 | tf_op jit(solution)/shard_map/shc,cl->shl/dot_general | solution.py:149
  245.0 2.4 fusion.22
  249.3 2.4 fusion.24
  253.1 2.6 fusion.26
  256.2 2.5 pad_maximum_fusion
  258.8 2.5 select_reduce_fusion.9
  261.3 28.7 %all-gather = f32[16,4,128]{2,1,0:T(4,128)S(1)} all-gather(f32[4,4,128]{2,1,0:T(4,128)S(1)} %pad_maximum_fusion.2), channel_id=2, replica_groups=mesh['side'=2,'owner'=32,'seq'=2] {'side','seq'}, dimensions={0}, use_global_device_ids=true | all-gather | bytes 40960 | tf_op jit(solution)/shard_map/all_gather | solution.py:13
  290.1 5.8 %fusion.11 = f32[4,128]{1,0:T(4,128)S(1)} fusion(f32[4,128,4096]{2,1,0:T(8,128)} %get-tuple-element.262, f32[4,128]{1,0:T(4,128)S(1)} %max.87, pred[4096]{0:T(1024)(128)(4,1)S(1)} %get-tuple-element.279), kind=kLoop, calls=%fused_computation.27 | loop fusion | flops 8388096 | bytes 8396800 | tf_op jit(solution)/shard_map/reduce_sum | solution.py:148
  296.0 5.0 %fusion.9 = f32[4,128]{1,0:T(4,128)S(1)} fusion(f32[4,128,4096]{2,1,0:T(8,128)} %get-tuple-element.266, f32[4,128]{1,0:T(4,128)S(1)} %max.85, pred[4096]{0:T(1024)(128)(4,1)S(1)} %get-tuple-element.280), kind=kLoop, calls=%fused_computation.25 | loop fusion | flops 8388096 | bytes 8396800 | tf_op jit(solution)/shard_map/reduce_sum | solution.py:148
  301.3 2.1 fusion.7
  303.7 2.1 fusion.5
  305.9 5.5 %all-gather.1 = f32[16,4,128]{2,1,0:T(4,128)S(1)} all-gather(f32[4,4,128]{2,1,0:T(4,128)S(1)} %pad_maximum_fusion.3), channel_id=3, replica_groups=mesh['side'=2,'owner'=32,'seq'=2] {'side','seq'}, dimensions={0}, use_global_device_ids=true | all-gather | bytes 40960 | tf_op jit(solution)/shard_map/all_gather | solution.py:13
  311.4 117.9 %all-gather.5.cloned.1.call-done = f32[16,4,128,512]{3,2,0,1:T(8,128)} async-done(((f32[4,4,128,512]{3,2,0,1:T(8,128)}), f32[16,4,128,512]{3,2,0,1:T(8,128)}) %all-gather.5.cloned.1.call-update) | async-done | bytes 16777232 | tf_op jit(solution)/shard_map/all_gather | solution.py:13
  429.3 2.2 slice-done
  431.5 2.6 copy.139
  434.1 15.5 %while.19 = (s32[]{:T(128)}, f32[4,4,128]{2,1,0:T(4,128)S(1)}, f32[4,4,128]{2,1,0:T(4,128)S(1)}, f32[4,4,128,512]{3,2,1,0:T(8,128)}, f32[4,4,4,128]{3,2,1,0:T(4,...) while((s32[]{:T(128)}, f32[4,4,128]{2,1,0:T(4,128)S(1)}, ...), condition=%wide.region_25.26_spmd, body=%wide.region_24.25_spmd.sunk | while | flops 3158021 | bytes 12664983 | solution.py:19
  434.2 5.2 %fusion.143 = f32[4,4,128,512]{3,2,1,0:T(8,128)} fusion(f32[4,4,128,512]{3,2,1,0:T(8,128)} %get-tuple-element.347, f32[4,4,128]{2,1,0:T(4,128)S(1)} %get-tuple-element.332, f32[4,4,128]{2,1,0:T(4,128)S(1)} %get-tuple-element.333, f32[4,4,4,128,512]{4,3,1,0,2:T(8,128)} %get-tuple-element.360, s32[]{:T(128)S(6)} %select_n.284), kind=kLoop, calls=%fused_computation.4.clone.1 | loop fusion | flops 3145728 | bytes 12599300 | tf_op jit(solution)/shard_map/while/body/eval_jaxpr/add | solution.py:70
  439.3 5.2 %fusion.143 = f32[4,4,128,512]{3,2,1,0:T(8,128)} fusion(f32[4,4,128,512]{3,2,1,0:T(8,128)} %get-tuple-element.347, f32[4,4,128]{2,1,0:T(4,128)S(1)} %get-tuple-element.332, f32[4,4,128]{2,1,0:T(4,128)S(1)} %get-tuple-element.333, f32[4,4,4,128,512]{4,3,1,0,2:T(8,128)} %get-tuple-element.360, s32[]{:T(128)S(6)} %select_n.284), kind=kLoop, calls=%fused_computation.4.clone.1 | loop fusion | flops 3145728 | bytes 12599300 | tf_op jit(solution)/shard_map/while/body/eval_jaxpr/add | solution.py:70
  444.5 5.2 %fusion.143 = f32[4,4,128,512]{3,2,1,0:T(8,128)} fusion(f32[4,4,128,512]{3,2,1,0:T(8,128)} %get-tuple-element.347, f32[4,4,128]{2,1,0:T(4,128)S(1)} %get-tuple-element.332, f32[4,4,128]{2,1,0:T(4,128)S(1)} %get-tuple-element.333, f32[4,4,4,128,512]{4,3,1,0,2:T(8,128)} %get-tuple-element.360, s32[]{:T(128)S(6)} %select_n.284), kind=kLoop, calls=%fused_computation.4.clone.1 | loop fusion | flops 3145728 | bytes 12599300 | tf_op jit(solution)/shard_map/while/body/eval_jaxpr/add | solution.py:70
  (159 shorter events, 24.6 us)
Async XLA Ops:
  6.5 190.1 %reduce-scatter.4.cloned.1.call-start = ((), (), s32[]{:S(2)}) async-start(), calls=%async_computation.4 | async-start | bytes 5406720
  20.2 19.6 %copy-start.7 = (s32[4]{0:T(128)S(1)}, s32[4]{0:T(128)}, u32[]{:S(2)}) copy-start(s32[4]{0:T(128)} %param.15) | copy-start | bytes 52
  20.2 19.8 %copy-start.3 = (s32[4]{0:T(128)S(1)}, s32[4]{0:T(128)}, u32[]{:S(2)}) copy-start(s32[4]{0:T(128)} %param.19) | copy-start | bytes 52
  28.3 54.6 %all-to-all-start = ((s32[32,1,8]{2,1,0:T(1,128)}), s32[32,1,8]{2,1,0:T(1,128)S(1)}, u32[]{:S(2)}, u32[]{:S(2)}) async-start(s32[32,1,8]{2,1,0:T(1,128)} %copy.120), calls=%async_computation | async-start | bytes 32768 | tf_op jit(solution)/shard_map/all_to_all | solution.py:119
  43.4 9.7 %copy-start.6 = (bf16[4,4,128,576]{2,3,1,0:T(8,128)(2,1)S(1)}, bf16[4,4,128,576]{2,3,1,0:T(8,128)(2,1)}, u32[]{:S(2)}) copy-start(bf16[4,4,128,576]{2,3,1,0:T(8,128)(2,1)} %param.20) | copy-start | bytes 7077892
  43.4 26.8 %slice-start.1 = ((s8[18874368]{0:T(1024)(128)(4,1)}), s8[4194304]{0:T(1024)(128)(4,1)S(1)}, s32[]{:S(2)}) async-start(s8[18874368]{0:T(1024)(128)(4,1)} %bitcast.235), calls=%async_computation.6 | async-start | bytes 8388608
  43.4 26.8 %slice-start.2 = ((s8[18874368]{0:T(1024)(128)(4,1)}), s8[4194304]{0:T(1024)(128)(4,1)S(1)}, s32[]{:S(2)}) async-start(s8[18874368]{0:T(1024)(128)(4,1)} %bitcast.235), calls=%async_computation.7 | async-start | bytes 8388608
  53.1 17.1 %slice-start.3 = ((s8[18874368]{0:T(1024)(128)(4,1)}), s8[4194304]{0:T(1024)(128)(4,1)S(1)}, s32[]{:S(2)}) async-start(s8[18874368]{0:T(1024)(128)(4,1)} %bitcast.235), calls=%async_computation.8 | async-start | bytes 8388608
  53.1 17.1 %slice-start.4 = ((s8[18874368]{0:T(1024)(128)(4,1)}), s8[4194304]{0:T(1024)(128)(4,1)S(1)}, s32[]{:S(2)}) async-start(s8[18874368]{0:T(1024)(128)(4,1)} %bitcast.235), calls=%async_computation.9 | async-start | bytes 8388608
  61.6 8.6 %slice-start.5 = ((s8[18874368]{0:T(1024)(128)(4,1)}), s8[2097152]{0:T(1024)(128)(4,1)S(1)}, s32[]{:S(2)}) async-start(s8[18874368]{0:T(1024)(128)(4,1)} %bitcast.235), calls=%async_computation.10 | async-start | bytes 4194304
  76.3 121.7 %copy-start.4 = (f32[512]{0:T(512)S(1)}, f32[512]{0:T(512)}, u32[]{:S(2)}) copy-start(f32[512]{0:T(512)} %param.14) | copy-start | bytes 6148
  216.4 14.4 %all-to-all-start.1 = ((bf16[32,8,576]{2,1,0:T(8,128)(2,1)}), bf16[32,8,576]{2,1,0:T(8,128)(2,1)S(1)}, u32[]{:S(2)}, u32[]{:S(2)}) async-start(bf16[32,8,576]{2,1,0:T(8,128)(2,1)} %scatter_fusion.1), calls=%async_computation.1 | async-start | bytes 655360 | tf_op jit(solution)/shard_map/all_to_all | solution.py:118
  220.7 208.6 %all-gather.5.cloned.1.call-start = ((), (), s32[]{:S(2)}) async-start(), calls=%async_computation.3 | async-start | bytes 20971520 | tf_op jit(solution)/shard_map/all_gather | solution.py:13
  234.4 10.5 %slice-start.14 = ((s8[8388608]{0:T(1024)(128)(4,1)}), s8[4194304]{0:T(1024)(128)(4,1)S(1)}, s32[]{:S(2)}) async-start(s8[8388608]{0:T(1024)(128)(4,1)} %bitcast.245), calls=%async_computation.19 | async-start | bytes 8388608
  235.9 9.1 %slice-start.20 = ((s8[4718592]{0:T(1024)(128)(4,1)}), s8[4194304]{0:T(1024)(128)(4,1)S(1)}, s32[]{:S(2)}) async-start(s8[4718592]{0:T(1024)(128)(4,1)} %bitcast.251), calls=%async_computation.25 | async-start | bytes 8388608
  237.4 7.6 %slice-start.15 = ((s8[8388608]{0:T(1024)(128)(4,1)}), s8[4194304]{0:T(1024)(128)(4,1)S(1)}, s32[]{:S(2)}) async-start(s8[8388608]{0:T(1024)(128)(4,1)} %bitcast.245), calls=%async_computation.20 | async-start | bytes 8388608
  237.4 7.6 %slice-start.21 = ((s8[4718592]{0:T(1024)(128)(4,1)}), s8[524288]{0:T(1024)(128)(4,1)S(1)}, s32[]{:S(2)}) async-start(s8[4718592]{0:T(1024)(128)(4,1)} %bitcast.251), calls=%async_computation.26 | async-start | bytes 1048576
  244.5 3.4 slice-start.10
  244.5 3.5 slice-start.18
  245.0 4.3 slice-start.11
  245.0 4.3 slice-start.19
  247.5 4.7 %slice-start.6 = ((s8[8388608]{0:T(1024)(128)(4,1)}), s8[4194304]{0:T(1024)(128)(4,1)S(1)}, s32[]{:S(2)}) async-start(s8[8388608]{0:T(1024)(128)(4,1)} %bitcast.237), calls=%async_computation.11 | async-start | bytes 8388608
  247.5 4.7 %slice-start.16 = ((s8[4718592]{0:T(1024)(128)(4,1)}), s8[4194304]{0:T(1024)(128)(4,1)S(1)}, s32[]{:S(2)}) async-start(s8[4718592]{0:T(1024)(128)(4,1)} %bitcast.247), calls=%async_computation.21 | async-start | bytes 8388608
  249.3 3.8 slice-start.7
  249.3 3.8 slice-start.17
  256.2 2.6 copy-start.2
  290.0 11.1 %slice-start.12 = ((s8[8388608]{0:T(1024)(128)(4,1)}), s8[4194304]{0:T(1024)(128)(4,1)S(1)}, s32[]{:S(2)}) async-start(s8[8388608]{0:T(1024)(128)(4,1)} %bitcast.243), calls=%async_computation.17 | async-start | bytes 8388608
  295.9 5.4 %slice-start.13 = ((s8[8388608]{0:T(1024)(128)(4,1)}), s8[4194304]{0:T(1024)(128)(4,1)S(1)}, s32[]{:S(2)}) async-start(s8[8388608]{0:T(1024)(128)(4,1)} %bitcast.243), calls=%async_computation.18 | async-start | bytes 8388608
  296.0 7.5 %slice-start.8 = ((s8[8388608]{0:T(1024)(128)(4,1)}), s8[4194304]{0:T(1024)(128)(4,1)S(1)}, s32[]{:S(2)}) async-start(s8[8388608]{0:T(1024)(128)(4,1)} %bitcast.239), calls=%async_computation.13 | async-start | bytes 8388608
  301.3 2.4 slice-start.9
  429.3 2.2 slice-start
  449.7 3.0 copy-start.1
  (2 other events, 2.2 us)
Sparse Core Ops, SparseCore 0:
  20.4 176.1 reduce-scatter.3
  258.9 170.3 all-gather.4
where the time goes:
time: 461 us; the launch traced here: 460 us
  waiting for transfers between devices  241 us (52%)
  matrix products  63.6 us (14%)
  local copies, waits for them, and re-layouts  53.9 us (12%)
  other arithmetic  37.3 us (8%)
  blocking collectives  34.2 us (7%)
  starting transfers between devices  16.1 us (3%)
  between operations  14.1 us (3%)
    all_gather x1, waiting for transfers between devices, joined(): everything = jax.tree.map(lambda part: lax.all_gather(part, axis), x)  118 us
    unnamed x3, waiting for transfers between devices  114 us
    all_gather x2, blocking collectives, joined(): everything = jax.tree.map(lambda part: lax.all_gather(part, axis), x)  34.2 us
    dot_general x4, matrix products, on_device(): jnp.einsum('shk,ck->shc', query_rows, cache_keys, preferred_element_type=...  32.8 us
    scatter x1, local copies, waits for them, and re-layouts, on_device(): outgoing = jnp.zeros((owners, capacity, key_width), jnp.bfloat16).at[targ...  17.3 us
    add x3, other arithmetic, join_partials(): first_part[2] * first_scale[..., None]  15.5 us
    reduce_sum x8, other arithmetic, on_device(): totals.append(jnp.sum(weights_cache, axis=2) + jnp.sum(weights_own, axis=2))  15.4 us
    dot_general x4, matrix products, on_device(): jnp.einsum('shc,cl->shl', weights_cache.astype(jnp.bfloat16), cache_keys[...  14.6 us
  transfers between devices with their start and end apart: 4, of which 3 were waited for; matrix products, arithmetic and copies ran while one was open for 15% of the time, Pallas kernels for 0%

commit v1 on v0

v1 whole, which is shorter than its diff:
```python
import functools

import jax
import jax.numpy as jnp
from jax import lax
from jax.experimental import pallas as pl
from jax.experimental.pallas import tpu as pltpu
from jax.sharding import PartitionSpec as P

rope_theta = 10000.0
norm_eps = 1e-06
masked_score = -1e30
score_scale = 192.0 ** (-0.5) * 1.4426950408889634

LATENT = 512
WIDTH = 576
EXT = 592
PAD = 640
HEADS = 128
KEYS = 4096
CHUNKS = 4
CHUNK = KEYS // CHUNKS
REQ = 4
ROWS = 512
PIECE = WIDTH // 4
RING_MASKS = (2, 8, 6, 24)
F32 = jnp.float32
BF16 = jnp.bfloat16


def piece_slot(piece, flips):
    slot = 0
    for i in range(4):
        slot = slot * 2 + ((flips >> ((piece + i) % 4)) & 1)
    return slot


def flips_mask(flips):
    mask = 0
    for i in range(4):
        if (flips >> i) & 1:
            mask ^= RING_MASKS[i]
    return mask


def kernel(
    lens_ref,
    plens_ref,
    hid_hbm,
    w_hbm,
    gain_ref,
    dest_ref,
    order_ref,
    cache_hbm,
    query_hbm,
    new_ref,
    out_ref,
    hid,
    w,
    wt,
    part,
    landed,
    keys,
    qraw,
    qx,
    qown,
    scores,
    tops,
    sums,
    acc,
    mstat,
    lstat,
    seq_acc,
    seq_m,
    seq_l,
    side_out,
    side_in,
    stat_out,
    stat_in,
    own_acc,
    own_m,
    own_l,
    ids,
    hand,
    outgoing,
    kown,
    in_sem,
    key_sem,
    rs_send,
    rs_recv,
    seq_send,
    seq_recv,
    side_send,
    side_recv,
    hand_send,
    hand_recv,
    a2a_send,
    a2a_recv,
    share_send,
    share_recv,
):
    side = lax.axis_index("side")
    owner = lax.axis_index("owner")
    seq = lax.axis_index("seq")
    quarter = side * 2 + seq
    y = owner % 2
    pair = owner // 2
    MESH = pl.DeviceIdType.MESH

    def flip(a, mask):
        out = a
        bit = 1
        while bit <= mask:
            if mask & bit:
                out = out + bit * (1 - 2 * ((a // bit) % 2))
            bit *= 2
        return out

    hid_copy = pltpu.make_async_copy(hid_hbm, hid, in_sem.at[0])
    w_copy = pltpu.make_async_copy(w_hbm, w, in_sem.at[1])
    q_copy = pltpu.make_async_copy(query_hbm, qraw, in_sem.at[2])

    def key_copy(r):
        return pltpu.make_async_copy(
            cache_hbm.at[r], keys.at[r % 2, pl.ds(0, WIDTH)], key_sem.at[r % 2]
        )

    hid_copy.start()
    w_copy.start()
    q_copy.start()
    key_copy(0).start()
    key_copy(1).start()

    seq_peer = (side, owner, 1 - seq)
    side_peer = (1 - side, owner, seq)
    rs_peers = [(side, flip(owner, mask), seq) for mask in RING_MASKS + (1,)]

    def a2a_target(i):
        k = i % 16
        there = (pair + k) % 16
        to_y = (y + seq) % 2
        to_side = (side + i // 16) % 2
        return (to_side, there * 2 + to_y, 1 - seq), there

    def a2a_source(i):
        k = i % 16
        there = (pair + 16 - k) % 16
        from_y = (y + 1 - seq) % 2
        from_side = (side + i // 16) % 2
        return (from_side, there * 2 + from_y, 1 - seq)

    barrier = pltpu.get_barrier_semaphore()
    for peer in rs_peers + [seq_peer, side_peer]:
        pl.semaphore_signal(barrier, inc=1, device_id=peer, device_id_type=MESH)

    def greet(i, _):
        pl.semaphore_signal(barrier, inc=1, device_id=a2a_source(i), device_id_type=MESH)
        return 0

    lax.fori_loop(0, 32, greet, 0)

    dest = dest_ref[:, pl.ds(pl.multiple_of(owner * 128, 128), 128)].astype(F32)
    dest_lane = jnp.broadcast_to(dest, (128, 128))
    dest_sub = dest_lane.T
    order_sub = jnp.broadcast_to(order_ref[...].astype(F32), (128, 128)).T
    sub = lax.broadcasted_iota(jnp.int32, (128, 128), 0)
    lane = lax.broadcasted_iota(jnp.int32, (128, 128), 1)
    slot = jnp.sum(jnp.where(order_sub == dest_lane, sub, 0), axis=0, keepdims=True)
    rank = jnp.sum(
        jnp.where((dest_sub == dest_lane) & (sub < lane), 1, 0), axis=0, keepdims=True
    )
    row_id = (slot // 4) * 16 + (slot % 4) * 4 + seq * 2 + rank
    ids[0] = jnp.broadcast_to(row_id, (8, 128))

    w_copy.wait()
    wt[...] = w[...].T
    hid_copy.wait()
    for flips in range(16):
        at = flip(owner, flips_mask(flips)) // 2
        block = jnp.dot(
            wt[...],
            hid[:, pl.ds(pl.multiple_of(at * 256, 256), 256)],
            preferred_element_type=F32,
        ).astype(BF16)
        for half in range(2):
            rel = (half + y) % 2
            for p in range(4):
                part[p, piece_slot(p, flips) * 2 + rel] = block[
                    p * PIECE : (p + 1) * PIECE, half * 128 : (half + 1) * 128
                ]

    pl.semaphore_wait(barrier, 7 + 32)

    id_copy = pltpu.make_async_remote_copy(
        ids.at[0], ids.at[1], hand_send.at[0], hand_recv.at[0], seq_peer, device_id_type=MESH
    )
    id_copy.start()

    starts = (0, 16, 24, 28, 30)

    def rs_copy(stage, p, sub_part):
        held = 32 >> stage
        if stage == 4:
            lo, n = 1, 1
            peer = rs_peers[4]
        else:
            n = held // 4
            lo = held // 2 + (n if sub_part == 0 else 0)
            peer = rs_peers[(p + stage) % 4]
        index = (stage * 2 + sub_part) * 4 + p
        return pltpu.make_async_remote_copy(
            part.at[p, pl.ds(lo, n)],
            landed.at[p, pl.ds(starts[stage] + lo - held // 2, n)],
            rs_send.at[index],
            rs_recv.at[index],
            peer,
            device_id_type=MESH,
        )

    def rs_start(stage):
        for sub_part in range(2 if stage < 4 else 1):
            for p in range(4):
                rs_copy(stage, p, sub_part).start()

    def rs_take(stage, sub_part):
        held = 32 >> stage
        n = held // 4
        lo = n if sub_part == 0 else 0
        for p in range(4):
            rs_copy(stage, p, sub_part).wait_recv()

            def add(j, _):
                part[p, lo + j] = part[p, lo + j] + landed[p, starts[stage] + lo + j]
                return 0

            lax.fori_loop(0, n, add, 0)

    def rs_first(stage):
        rs_take(stage, 0)
        rs_start(stage + 1)

    def rs_second(stage):
        rs_take(stage, 1)

    rs_start(0)

    kown[1024:1152, :] = jnp.zeros((128, PAD), BF16)
    new_all = jnp.concatenate([new_ref[u].astype(F32) for u in range(4)], axis=0)
    kown[1024:1040, 0:WIDTH] = new_all.astype(BF16)
    marks = jnp.where(
        lax.broadcasted_iota(jnp.int32, (PAD - WIDTH, 128), 0) == 0, -1.0, 0.0
    ).astype(BF16)
    for c in range(2):
        hand[c, WIDTH:PAD, :] = marks

    q_copy.wait()

    def queries_in(r):
        lead = jnp.where(
            lax.broadcasted_iota(jnp.int32, (128, EXT - WIDTH), 1) == 0, masked_score, 0.0
        ).astype(BF16)
        for s in range(4):
            rows = qraw[s, r].T
            for hq in range(4):
                rel_seq = (hq + seq) % 2
                rel_side = (hq // 2 + side) % 2
                at = pl.multiple_of((rel_seq * 2 + rel_side) * 128 + s * 32, 32)
                qx[r % 2, pl.ds(at, 32), 0:WIDTH] = rows[hq * 32 : (hq + 1) * 32]
        for s in range(4):
            qx[r % 2, s * 128 : (s + 1) * 128, WIDTH:EXT] = lead
        qown[r * 128 : (r + 1) * 128, :] = qx[r % 2, 0:128, :]

    def dead_row(r):
        place = lax.broadcasted_iota(jnp.int32, (EXT - WIDTH, KEYS), 1) + quarter * KEYS
        first = lax.broadcasted_iota(jnp.int32, (EXT - WIDTH, KEYS), 0) == 0
        keys[r % 2, WIDTH:EXT, :] = jnp.where(
            (place >= lens_ref[r]) & first, 1.0, 0.0
        ).astype(BF16)

    def seq_copies(r):
        return [
            pltpu.make_async_remote_copy(
                src.at[r, pl.ds(256, 256)],
                dst.at[r],
                seq_send.at[r * 3 + i],
                seq_recv.at[r * 3 + i],
                seq_peer,
                device_id_type=MESH,
            )
            for i, (src, dst) in enumerate(((acc, seq_acc), (mstat, seq_m), (lstat, seq_l)))
        ]

    def side_copies(r):
        return [
            pltpu.make_async_remote_copy(
                src.at[r],
                dst.at[r],
                side_send.at[r * 2 + i],
                side_recv.at[r * 2 + i],
                side_peer,
                device_id_type=MESH,
            )
            for i, (src, dst) in enumerate(((side_out, side_in), (stat_out, stat_in)))
        ]

    def seq_start(r):
        total = jnp.sum(sums[...], axis=1, keepdims=True)
        lstat[r] = jnp.broadcast_to(total, (ROWS, 128))
        for copy in seq_copies(r):
            copy.start()

    def wide(x):
        return jnp.concatenate([x] * 4, axis=1)

    def seq_join(r):
        for copy in seq_copies(r):
            copy.wait_recv()
        for half in (1, 0):
            rows = pl.ds(half * 128, 128)
            m_a, m_b = mstat[r, rows], seq_m[r, rows]
            top = jnp.maximum(m_a, m_b)
            e_a, e_b = jnp.exp2(m_a - top), jnp.exp2(m_b - top)
            total = lstat[r, rows] * e_a + seq_l[r, rows] * e_b
            joined = acc[r, rows] * wide(e_a) + seq_acc[r, rows] * wide(e_b)
            if half == 1:
                side_out[r] = joined.astype(BF16)
                eight = lax.broadcasted_iota(jnp.int32, (8, 128), 0)
                stat_out[r] = jnp.where(eight < 4, top.T[0:8], total.T[0:8])
                for copy in side_copies(r):
                    copy.start()
            else:
                own_acc[r] = joined
                own_m[r] = top
                own_l[r] = total

    def side_join(r):
        for copy in side_copies(r):
            copy.wait_recv()
        m_a = own_m[r]
        m_b = jnp.broadcast_to(stat_in[r, 0:1], (128, 128)).T
        l_b = jnp.broadcast_to(stat_in[r, 4:5], (128, 128)).T
        top = jnp.maximum(m_a, m_b)
        e_a, e_b = jnp.exp2(m_a - top), jnp.exp2(m_b - top)
        own_l[r] = own_l[r] * e_a + l_b * e_b
        own_m[r] = top
        own_acc[r] = own_acc[r] * wide(e_a) + side_in[r].astype(F32) * wide(e_b)

    def handed():
        rows = []
        for p in range(4):
            rs_copy(4, p, 0).wait_recv()
            rows.append(part[p, 0].astype(F32) + landed[p, starts[4]].astype(F32))
        row = jnp.concatenate(rows, axis=0)
        latent = row[0:LATENT]
        mean = jnp.sum(latent * latent, axis=0, keepdims=True) * (1.0 / LATENT)
        gain = jnp.broadcast_to(gain_ref[...], (128, LATENT)).T
        hand[0, 0:LATENT, :] = (latent * lax.rsqrt(mean + norm_eps) * gain).astype(BF16)
        token = (
            quarter * 4096 + owner * 128 + lax.broadcasted_iota(jnp.int32, (32, 128), 1)
        )
        began = jnp.zeros((32, 128), jnp.int32)
        start = jnp.int32(0)
        for p in range(4):
            began = jnp.maximum(began, jnp.where(start <= token, start, 0))
            start = start + plens_ref[p]
        which = lax.broadcasted_iota(jnp.int32, (32, 128), 0)
        frequency = jnp.ones((32, 128), F32)
        for i in range(1, 32):
            frequency = jnp.where(which == i, rope_theta ** (-i / 32), frequency)
        angle = (token - began).astype(F32) * frequency
        cosine, sine = jnp.cos(angle), jnp.sin(angle)
        b, c = row[LATENT : LATENT + 32], row[LATENT + 32 : WIDTH]
        hand[0, LATENT : LATENT + 32, :] = (b * cosine - c * sine).astype(BF16)
        hand[0, LATENT + 32 : WIDTH, :] = (b * sine + c * cosine).astype(BF16)

    hand_copy = pltpu.make_async_remote_copy(
        hand.at[0, pl.ds(0, WIDTH)],
        hand.at[1, pl.ds(0, WIDTH)],
        hand_send.at[1],
        hand_recv.at[1],
        seq_peer,
        device_id_type=MESH,
    )

    def pack_rows():
        packed = jnp.where(lax.broadcasted_iota(jnp.int32, (256, PAD), 1) == WIDTH, 1.0, 0.0)
        to_y = (y + seq) % 2
        for c in range(2):
            group = ids[c, 0:1] // 16
            place = jnp.where(group % 2 == to_y, (group // 2) * 16 + ids[c, 0:1] % 16, -1)
            hot = jnp.where(
                lax.broadcasted_iota(jnp.int32, (256, 128), 0) == place, 1.0, 0.0
            ).astype(BF16)
            packed = packed + lax.dot_general(
                hot, hand[c], (((1,), (1,)), ((), ())), preferred_element_type=F32
            )
        outgoing[...] = packed.astype(BF16)

    def a2a_copy(i):
        device, there = a2a_target(i)
        return pltpu.make_async_remote_copy(
            outgoing.at[pl.ds(pl.multiple_of(there * 16, 16), 16)],
            kown.at[pl.ds(pl.multiple_of(i * 16, 16), 16)],
            a2a_send.at[i],
            a2a_recv.at[i],
            device,
            device_id_type=MESH,
        )

    def share_copy(i):
        return pltpu.make_async_remote_copy(
            kown.at[pl.ds(i * 256, 256)],
            kown.at[pl.ds(512 + i * 256, 256)],
            share_send.at[i],
            share_recv.at[i],
            seq_peer,
            device_id_type=MESH,
        )

    def loop(lo, hi, f):
        def step(i, _):
            f(i)
            return 0

        lax.fori_loop(lo, hi, step, 0)

    hooks = {
        (1, 2): [lambda: rs_first(0)],
        (2, 1): [lambda: rs_second(0)],
        (2, 2): [lambda: seq_join(0)],
        (2, 3): [lambda: rs_first(1)],
        (3, 0): [lambda: rs_second(1)],
        (3, 1): [lambda: rs_first(2)],
        (3, 2): [lambda: rs_second(2), lambda: rs_first(3), lambda: seq_join(1)],
        (3, 3): [lambda: rs_second(3)],
        (4, 2): [lambda: seq_join(2)],
    }

    for r in range(REQ + 1):
        if r < REQ:
            queries_in(r)
            dead_row(r)
            tops[r % 2] = jnp.full((ROWS, 128), -3e38, F32)
            key_copy(r).wait()
        if r > 0:
            b = r - 1
            top = jnp.max(tops[b % 2], axis=1, keepdims=True) * score_scale
            mstat[b] = jnp.broadcast_to(top, (ROWS, 128))
            sums[...] = jnp.zeros((ROWS, 128), F32)
            acc[b] = jnp.zeros((ROWS, LATENT), F32)

        def chunk(c, _):
            for (hook_r, hook_c), acts in hooks.items():
                if hook_r == r:

                    @pl.when(c == hook_c)
                    def _():
                        for act in acts:
                            act()

            at = pl.ds(pl.multiple_of(c * CHUNK, CHUNK), CHUNK)
            if r < REQ:
                fresh = jnp.dot(qx[r % 2], keys[r % 2, :, at], preferred_element_type=F32)
                scores[r % 2, :, at] = fresh
                top = tops[r % 2]
                for j in range(CHUNK // 128):
                    top = jnp.maximum(top, fresh[:, j * 128 : (j + 1) * 128])
                tops[r % 2] = top
            if r > 0:
                b = r - 1
                m = mstat[b]
                ready = scores[b % 2, :, at]
                weights = [
                    jnp.exp2(ready[:, j * 128 : (j + 1) * 128] * score_scale - m)
                    for j in range(CHUNK // 128)
                ]
                sums[...] += functools.reduce(jnp.add, weights)
                acc[b] += lax.dot_general(
                    jnp.concatenate(weights, axis=1).astype(BF16),
                    keys[b % 2, 0:LATENT, at],
                    (((1,), (1,)), ((), ())),
                    preferred_element_type=F32,
                )
            return 0

        lax.fori_loop(0, CHUNKS, chunk, 0)
        if r > 0:
            seq_start(r - 1)
            if r + 1 < REQ:
                key_copy(r + 1).start()

    handed()
    hand_copy.start()
    seq_join(3)
    side_join(0)
    id_copy.wait_recv()
    hand_copy.wait_recv()
    pack_rows()
    loop(0, 32, lambda i: a2a_copy(i).start())
    side_join(1)
    side_join(2)
    side_join(3)
    loop(0, 16, lambda i: a2a_copy(i).wait_recv())
    share_copy(0).start()
    loop(16, 32, lambda i: a2a_copy(i).wait_recv())
    share_copy(1).start()
    share_copy(0).wait_recv()
    share_copy(1).wait_recv()

    own_scores = lax.dot_general(
        qown[...], kown[:, 0:EXT], (((1,), (1,)), ((), ())), preferred_element_type=F32
    )
    column = lax.broadcasted_iota(jnp.int32, (1, 1024), 1)
    new_column = lax.broadcasted_iota(jnp.int32, (128, 128), 1)
    new_step = lax.broadcasted_iota(jnp.int32, (128, 128), 0) // 32
    for r in range(REQ):
        rows = own_scores[r * 128 : (r + 1) * 128]
        old = jnp.where((column // 4) % 4 == r, rows[:, 0:1024], masked_score)
        live = (new_column < 16) & (new_column % 4 == r) & (new_column // 4 <= new_step)
        late = jnp.where(live, rows[:, 1024:1152], masked_score)
        everything = jnp.concatenate([old, late], axis=1) * score_scale
        m_b = jnp.max(everything, axis=1, keepdims=True)
        weights = jnp.exp2(everything - m_b)
        l_b = jnp.sum(weights, axis=1, keepdims=True)
        acc_b = jnp.dot(weights.astype(BF16), kown[:, 0:LATENT], preferred_element_type=F32)
        m_a = own_m[r][:, 0:1]
        l_a = own_l[r][:, 0:1]
        top = jnp.maximum(m_a, m_b)
        e_a, e_b = jnp.exp2(m_a - top), jnp.exp2(m_b - top)
        total = l_a * e_a + l_b * e_b
        result = (own_acc[r] * e_a + acc_b * e_b) / total
        for s in range(4):
            out_ref[s, r] = result[s * 32 : (s + 1) * 32].astype(BF16)

    for stage in range(5):
        for sub_part in range(2 if stage < 4 else 1):
            for p in range(4):
                rs_copy(stage, p, sub_part).wait_send()
    for r in range(REQ):
        for copy in seq_copies(r) + side_copies(r):
            copy.wait_send()
    id_copy.wait_send()
    hand_copy.wait_send()
    loop(0, 32, lambda i: a2a_copy(i).wait_send())
    share_copy(0).wait_send()
    share_copy(1).wait_send()


def on_device(
    prompt_hidden,
    latent_weight,
    kv_gain,
    prompt_lengths,
    destination,
    request_order,
    cache,
    cache_lengths,
    queries,
    new_rows,
):
    smem = pl.BlockSpec(memory_space=pltpu.SMEM)
    vmem = pl.BlockSpec(memory_space=pltpu.VMEM)
    hbm = pl.BlockSpec(memory_space=pl.ANY)
    dma = pltpu.SemaphoreType.DMA
    return pl.pallas_call(
        kernel,
        out_shape=jax.ShapeDtypeStruct((4, 4, 32, LATENT), BF16),
        in_specs=[smem, smem, hbm, hbm, vmem, vmem, vmem, hbm, hbm, vmem],
        out_specs=vmem,
        scratch_shapes=[
            pltpu.VMEM((224, 4096), BF16),
            pltpu.VMEM((224, WIDTH), BF16),
            pltpu.VMEM((WIDTH, 224), BF16),
            pltpu.VMEM((4, 32, PIECE, 128), BF16),
            pltpu.VMEM((4, 31, PIECE, 128), BF16),
            pltpu.VMEM((2, EXT, KEYS), BF16),
            pltpu.VMEM((4, 4, WIDTH, HEADS), BF16),
            pltpu.VMEM((2, ROWS, EXT), BF16),
            pltpu.VMEM((ROWS, EXT), BF16),
            pltpu.VMEM((2, ROWS, KEYS), F32),
            pltpu.VMEM((2, ROWS, 128), F32),
            pltpu.VMEM((ROWS, 128), F32),
            pltpu.VMEM((REQ, ROWS, LATENT), F32),
            pltpu.VMEM((REQ, ROWS, 128), F32),
            pltpu.VMEM((REQ, ROWS, 128), F32),
            pltpu.VMEM((REQ, 256, LATENT), F32),
            pltpu.VMEM((REQ, 256, 128), F32),
            pltpu.VMEM((REQ, 256, 128), F32),
            pltpu.VMEM((REQ, 128, LATENT), BF16),
            pltpu.VMEM((REQ, 128, LATENT), BF16),
            pltpu.VMEM((REQ, 8, 128), F32),
            pltpu.VMEM((REQ, 8, 128), F32),
            pltpu.VMEM((REQ, 128, LATENT), F32),
            pltpu.VMEM((REQ, 128, 128), F32),
            pltpu.VMEM((REQ, 128, 128), F32),
            pltpu.VMEM((2, 8, 128), jnp.int32),
            pltpu.VMEM((2, PAD, 128), BF16),
            pltpu.VMEM((256, PAD), BF16),
            pltpu.VMEM((1152, PAD), BF16),
            dma((3,)),
            dma((2,)),
            dma((36,)),
            dma((36,)),
            dma((12,)),
            dma((12,)),
            dma((8,)),
            dma((8,)),
            dma((2,)),
            dma((2,)),
            dma((32,)),
            dma((32,)),
            dma((2,)),
            dma((2,)),
        ],
        compiler_params=pltpu.CompilerParams(
            collective_id=0, has_side_effects=True, vmem_limit_bytes=62 << 20
        ),
        cost_estimate=pl.CostEstimate(
            flops=20_000_000_000, bytes_accessed=24_000_000, transcendentals=8_400_000
        ),
    )(
        cache_lengths,
        prompt_lengths,
        prompt_hidden.T,
        latent_weight,
        kv_gain.reshape(1, LATENT),
        destination.T,
        request_order.reshape(1, 128),
        jnp.transpose(cache, (0, 2, 1)),
        jnp.transpose(queries, (0, 1, 3, 2)),
        new_rows,
    )


def solution(mesh):
    return jax.shard_map(
        on_device,
        mesh=mesh,
        in_specs=(
            P(("side", "seq"), "owner"),
            P("owner", None),
            P(),
            P(),
            P(("side", "seq"), None),
            P(),
            P("owner", ("side", "seq"), None),
            P("owner"),
            P(None, "owner", None, None),
            P(None, "owner", None),
        ),
        out_specs=P(None, "owner", ("side", "seq"), None),
        check_vma=False,
    )
```

time: 461 us -> 73.8 us (0.16)
  waiting for transfers between devices: 241 us -> 0 us
  Pallas kernels: 0 us -> 71.6 us
  matrix products: 63.6 us -> 0 us
  local copies, waits for them, and re-layouts: 53.9 us -> 1.88 us
  other arithmetic: 37.3 us -> 0 us
  blocking collectives: 34.2 us -> 0 us
  starting transfers between devices: 16.1 us -> 0 us
  between operations: 14.1 us -> 0.01 us
    all_gather x1 -> x0, waiting for transfers between devices: 118 us -> none  [joined(): everything = jax.tree.map(lambda part: lax.all_gather(part, axis), x)]
    unnamed x3 -> x0, waiting for transfers between devices: 114 us -> none
    pallas_call x0 -> x1, Pallas kernels: none -> 71.6 us  [on_device(): pl.pallas_call(kernel, out_shape=jax.ShapeDtypeStruct((4, 4, 32, LATENT),...]
    dot_general x19 -> x0, matrix products: 63.6 us -> none  [the longest x4 32.8 us: on_device(): jnp.einsum('shk,ck->shc', query_rows, cache_keys, preferred_element_type=...]
    all_gather x2 -> x0, blocking collectives: 34.2 us -> none  [joined(): everything = jax.tree.map(lambda part: lax.all_gather(part, axis), x)]
    scatter x2 -> x0, local copies, waits for them, and re-layouts: 23.8 us -> none  [the longest x1 17.3 us: on_device(): outgoing = jnp.zeros((owners, capacity, key_width), jnp.bfloat16).at[targ...]
    all_to_all x2 -> x0, starting transfers between devices: 15.8 us -> none  [the longest x1 11.5 us: on_device(): lax.all_to_all(marks, 'owner', split_axis=0, concat_axis=0, tiled=True)]
    reduce_sum x11 -> x0, other arithmetic: 15.8 us -> none  [the longest x8 15.4 us: on_device(): totals.append(jnp.sum(weights_cache, axis=2) + jnp.sum(weights_own, axis=2))]
  transfers between devices with their start and end apart: 4 -> 0, of which waited for: 3 -> 0; matrix products, arithmetic and copies ran while one was open for 15% -> 0% of each run, Pallas kernels for 0% -> 0%
where the time goes in v1:
time: 73.8 us; the launch traced here: 73.5 us
  Pallas kernels  71.6 us (97%)
  local copies, waits for them, and re-layouts  1.88 us (3%)
    pallas_call x1, Pallas kernels, on_device(): pl.pallas_call(kernel, out_shape=jax.ShapeDtypeStruct((4, 4, 32, LATENT),...  71.6 us
    unnamed x1, local copies, waits for them, and re-layouts  1.88 us

profile of v1, /device:TPU:1, one launch (start us, length us, event | category | flops | bytes accessed | tf_op | source)
XLA Modules:
  0.0 73.5 jit_solution(12819461284776578852)
XLA Ops:
  0.0 71.6 %shard_map.100 = bf16[4,4,32,512]{3,2,1,0:T(8,128)(2,1)} custom-call(s32[4]{0:T(128)} %lens_ref.1, s32[4]{0:T(128)} %plens_ref.1, bf16[224,4096]{1,0:T(8,128)(2,1)} %bitcast.8, bf16[224,576]{1,0:T(8,128)(2,1)} %w_hbm.1, f32[1,512]{1,0:T(1,128)} %bitcast.10, s32[1,4096]{1,0:T(1,128)} %bitcast.9, s32[1,128]{1,0:T(1,128)} %bitcast.11, ...), custom_call_target="tpu_custom_call" | custom-call | flops 20000000000 | bytes 24000000 | tf_op jit(solution)/shard_map/pallas_call | solution.py:565
  71.6 1.9 %copy.12 = bf16[4,4,32,512]{3,2,1,0:T(8,128)(2,1)} copy(bf16[4,4,32,512]{3,2,1,0:T(8,128)(2,1)} %shard_map.100) | data formatting | bytes 1048576

commit v2 on v1

--- a/solution.py
+++ b/solution.py
@@ -18,11 +18,13 @@
 PAD = 640
 HEADS = 128
 KEYS = 4096
-CHUNKS = 4
-CHUNK = KEYS // CHUNKS
+CHUNKS = (4, 4, 4, 8, 8)
+CUTS = (4, 6)
 REQ = 4
 ROWS = 512
 PIECE = WIDTH // 4
+NEW = 512
+OTHER = NEW + 128
 RING_MASKS = (2, 8, 6, 24)
 F32 = jnp.float32
 BF16 = jnp.bfloat16
@@ -70,9 +72,10 @@
     acc,
     mstat,
     lstat,
-    seq_acc,
-    seq_m,
-    seq_l,
+    seq_out,
+    seq_in,
+    seq_stat,
+    seq_stat_in,
     side_out,
     side_in,
     stat_out,
@@ -84,6 +87,9 @@
     hand,
     outgoing,
     kown,
+    gain_wide,
+    turn,
+    hot,
     in_sem,
     key_sem,
     rs_send,
@@ -98,6 +104,7 @@
     a2a_recv,
     share_send,
     share_recv,
+    ready,
 ):
     side = lax.axis_index("side")
     owner = lax.axis_index("owner")
@@ -116,21 +123,6 @@
             bit *= 2
         return out
 
-    hid_copy = pltpu.make_async_copy(hid_hbm, hid, in_sem.at[0])
-    w_copy = pltpu.make_async_copy(w_hbm, w, in_sem.at[1])
-    q_copy = pltpu.make_async_copy(query_hbm, qraw, in_sem.at[2])
-
-    def key_copy(r):
-        return pltpu.make_async_copy(
-            cache_hbm.at[r], keys.at[r % 2, pl.ds(0, WIDTH)], key_sem.at[r % 2]
-        )
-
-    hid_copy.start()
-    w_copy.start()
-    q_copy.start()
-    key_copy(0).start()
-    key_copy(1).start()
-
     seq_peer = (side, owner, 1 - seq)
     side_peer = (1 - side, owner, seq)
     rs_peers = [(side, flip(owner, mask), seq) for mask in RING_MASKS + (1,)]
@@ -142,22 +134,22 @@
         to_side = (side + i // 16) % 2
         return (to_side, there * 2 + to_y, 1 - seq), there
 
-    def a2a_source(i):
-        k = i % 16
-        there = (pair + 16 - k) % 16
-        from_y = (y + 1 - seq) % 2
-        from_side = (side + i // 16) % 2
-        return (from_side, there * 2 + from_y, 1 - seq)
-
     barrier = pltpu.get_barrier_semaphore()
     for peer in rs_peers + [seq_peer, side_peer]:
         pl.semaphore_signal(barrier, inc=1, device_id=peer, device_id_type=MESH)
 
-    def greet(i, _):
-        pl.semaphore_signal(barrier, inc=1, device_id=a2a_source(i), device_id_type=MESH)
-        return 0
-
-    lax.fori_loop(0, 32, greet, 0)
+
+    hid_copy = pltpu.make_async_copy(hid_hbm, hid, in_sem.at[0])
+    w_copy = pltpu.make_async_copy(w_hbm, w, in_sem.at[1])
+    q_copy = pltpu.make_async_copy(query_hbm, qraw, in_sem.at[2])
+
+    def key_copy(r):
+        return pltpu.make_async_copy(
+            cache_hbm.at[r], keys.at[r % 2, pl.ds(0, WIDTH)], key_sem.at[r % 2]
+        )
+
+    w_copy.start()
+    hid_copy.start()
 
     dest = dest_ref[:, pl.ds(pl.multiple_of(owner * 128, 128), 128)].astype(F32)
     dest_lane = jnp.broadcast_to(dest, (128, 128))
@@ -175,7 +167,11 @@
     w_copy.wait()
     wt[...] = w[...].T
     hid_copy.wait()
-    for flips in range(16):
+    q_copy.start()
+    key_copy(0).start()
+    key_copy(1).start()
+
+    def project(flips):
         at = flip(owner, flips_mask(flips)) // 2
         block = jnp.dot(
             wt[...],
@@ -188,13 +184,6 @@
                 part[p, piece_slot(p, flips) * 2 + rel] = block[
                     p * PIECE : (p + 1) * PIECE, half * 128 : (half + 1) * 128
                 ]
-
-    pl.semaphore_wait(barrier, 7 + 32)
-
-    id_copy = pltpu.make_async_remote_copy(
-        ids.at[0], ids.at[1], hand_send.at[0], hand_recv.at[0], seq_peer, device_id_type=MESH
-    )
-    id_copy.start()
 
     starts = (0, 16, 24, 28, 30)
 
@@ -217,10 +206,14 @@
             device_id_type=MESH,
         )
 
+    def rs_part(stage, sub_part):
+        for p in range(4):
+            rs_copy(stage, p, sub_part).start()
+
     def rs_start(stage):
-        for sub_part in range(2 if stage < 4 else 1):
-            for p in range(4):
-                rs_copy(stage, p, sub_part).start()
+        rs_part(stage, 0)
+        if stage < 4:
+            rs_part(stage, 1)
 
     def rs_take(stage, sub_part):
         held = 32 >> stage
@@ -242,11 +235,21 @@
     def rs_second(stage):
         rs_take(stage, 1)
 
-    rs_start(0)
-
-    kown[1024:1152, :] = jnp.zeros((128, PAD), BF16)
+    for flips in (15, 7, 11, 13, 14, 3, 6, 12, 9):
+        project(flips)
+    pl.semaphore_wait(barrier, 7)
+    rs_part(0, 0)
+    for flips in (5, 10, 1, 2, 4, 8, 0):
+        project(flips)
+    rs_part(0, 1)
+    id_copy = pltpu.make_async_remote_copy(
+        ids.at[0], ids.at[1], hand_send.at[0], hand_recv.at[0], seq_peer, device_id_type=MESH
+    )
+    id_copy.start()
+
+    kown[NEW : NEW + 128, :] = jnp.zeros((128, PAD), BF16)
     new_all = jnp.concatenate([new_ref[u].astype(F32) for u in range(4)], axis=0)
-    kown[1024:1040, 0:WIDTH] = new_all.astype(BF16)
+    kown[NEW : NEW + 16, 0:WIDTH] = new_all.astype(BF16)
     marks = jnp.where(
         lax.broadcasted_iota(jnp.int32, (PAD - WIDTH, 128), 0) == 0, -1.0, 0.0
     ).astype(BF16)
@@ -280,15 +283,25 @@
     def seq_copies(r):
         return [
             pltpu.make_async_remote_copy(
-                src.at[r, pl.ds(256, 256)],
+                src.at[r],
                 dst.at[r],
-                seq_send.at[r * 3 + i],
-                seq_recv.at[r * 3 + i],
+                seq_send.at[r * 2 + i],
+                seq_recv.at[r * 2 + i],
                 seq_peer,
                 device_id_type=MESH,
             )
-            for i, (src, dst) in enumerate(((acc, seq_acc), (mstat, seq_m), (lstat, seq_l)))
+            for i, (src, dst) in enumerate(((seq_out, seq_in), (seq_stat, seq_stat_in)))
         ]
+
+    def compact(m, total):
+        eight = lax.broadcasted_iota(jnp.int32, (8, 128), 0)
+        return jnp.where(eight < 4, m.T[0:8], total.T[0:8])
+
+    def spread(tile):
+        return (
+            jnp.broadcast_to(tile[0:1], (128, 128)).T,
+            jnp.broadcast_to(tile[4:5], (128, 128)).T,
+        )
 
     def side_copies(r):
         return [
@@ -306,6 +319,10 @@
     def seq_start(r):
         total = jnp.sum(sums[...], axis=1, keepdims=True)
         lstat[r] = jnp.broadcast_to(total, (ROWS, 128))
+        for half in range(2):
+            rows = pl.ds(256 + half * 128, 128)
+            seq_out[r, half] = acc[r, rows].astype(BF16)
+            seq_stat[r, half] = compact(mstat[r, rows], lstat[r, rows])
         for copy in seq_copies(r):
             copy.start()
 
@@ -317,15 +334,15 @@
             copy.wait_recv()
         for half in (1, 0):
             rows = pl.ds(half * 128, 128)
-            m_a, m_b = mstat[r, rows], seq_m[r, rows]
+            m_a, l_a = mstat[r, rows], lstat[r, rows]
+            m_b, l_b = spread(seq_stat_in[r, half])
             top = jnp.maximum(m_a, m_b)
             e_a, e_b = jnp.exp2(m_a - top), jnp.exp2(m_b - top)
-            total = lstat[r, rows] * e_a + seq_l[r, rows] * e_b
-            joined = acc[r, rows] * wide(e_a) + seq_acc[r, rows] * wide(e_b)
+            total = l_a * e_a + l_b * e_b
+            joined = acc[r, rows] * wide(e_a) + seq_in[r, half].astype(F32) * wide(e_b)
             if half == 1:
                 side_out[r] = joined.astype(BF16)
-                eight = lax.broadcasted_iota(jnp.int32, (8, 128), 0)
-                stat_out[r] = jnp.where(eight < 4, top.T[0:8], total.T[0:8])
+                stat_out[r] = compact(top, total)
                 for copy in side_copies(r):
                     copy.start()
             else:
@@ -337,24 +354,15 @@
         for copy in side_copies(r):
             copy.wait_recv()
         m_a = own_m[r]
-        m_b = jnp.broadcast_to(stat_in[r, 0:1], (128, 128)).T
-        l_b = jnp.broadcast_to(stat_in[r, 4:5], (128, 128)).T
+        m_b, l_b = spread(stat_in[r])
         top = jnp.maximum(m_a, m_b)
         e_a, e_b = jnp.exp2(m_a - top), jnp.exp2(m_b - top)
         own_l[r] = own_l[r] * e_a + l_b * e_b
         own_m[r] = top
         own_acc[r] = own_acc[r] * wide(e_a) + side_in[r].astype(F32) * wide(e_b)
 
-    def handed():
-        rows = []
-        for p in range(4):
-            rs_copy(4, p, 0).wait_recv()
-            rows.append(part[p, 0].astype(F32) + landed[p, starts[4]].astype(F32))
-        row = jnp.concatenate(rows, axis=0)
-        latent = row[0:LATENT]
-        mean = jnp.sum(latent * latent, axis=0, keepdims=True) * (1.0 / LATENT)
-        gain = jnp.broadcast_to(gain_ref[...], (128, LATENT)).T
-        hand[0, 0:LATENT, :] = (latent * lax.rsqrt(mean + norm_eps) * gain).astype(BF16)
+    def before_handing():
+        gain_wide[...] = jnp.broadcast_to(gain_ref[...], (128, LATENT)).T
         token = (
             quarter * 4096 + owner * 128 + lax.broadcasted_iota(jnp.int32, (32, 128), 1)
         )
@@ -368,7 +376,29 @@
         for i in range(1, 32):
             frequency = jnp.where(which == i, rope_theta ** (-i / 32), frequency)
         angle = (token - began).astype(F32) * frequency
-        cosine, sine = jnp.cos(angle), jnp.sin(angle)
+        turn[0] = jnp.cos(angle)
+        turn[1] = jnp.sin(angle)
+
+    def places():
+        id_copy.wait_recv()
+        to_y = (y + seq) % 2
+        for c in range(2):
+            group = ids[c, 0:1] // 16
+            place = jnp.where(group % 2 == to_y, (group // 2) * 16 + ids[c, 0:1] % 16, -1)
+            hot[c] = jnp.where(
+                lax.broadcasted_iota(jnp.int32, (256, 128), 0) == place, 1.0, 0.0
+            ).astype(BF16)
+
+    def handed():
+        rows = []
+        for p in range(4):
+            rs_copy(4, p, 0).wait_recv()
+            rows.append(part[p, 0].astype(F32) + landed[p, starts[4]].astype(F32))
+        row = jnp.concatenate(rows, axis=0)
+        latent = row[0:LATENT]
+        mean = jnp.sum(latent * latent, axis=0, keepdims=True) * (1.0 / LATENT)
+        hand[0, 0:LATENT, :] = (latent * lax.rsqrt(mean + norm_eps) * gain_wide[...]).astype(BF16)
+        cosine, sine = turn[0], turn[1]
         b, c = row[LATENT : LATENT + 32], row[LATENT + 32 : WIDTH]
         hand[0, LATENT : LATENT + 32, :] = (b * cosine - c * sine).astype(BF16)
         hand[0, LATENT + 32 : WIDTH, :] = (b * sine + c * cosine).astype(BF16)
@@ -384,15 +414,9 @@
 
     def pack_rows():
         packed = jnp.where(lax.broadcasted_iota(jnp.int32, (256, PAD), 1) == WIDTH, 1.0, 0.0)
-        to_y = (y + seq) % 2
         for c in range(2):
-            group = ids[c, 0:1] // 16
-            place = jnp.where(group % 2 == to_y, (group // 2) * 16 + ids[c, 0:1] % 16, -1)
-            hot = jnp.where(
-                lax.broadcasted_iota(jnp.int32, (256, 128), 0) == place, 1.0, 0.0
-            ).astype(BF16)
             packed = packed + lax.dot_general(
-                hot, hand[c], (((1,), (1,)), ((), ())), preferred_element_type=F32
+                hot[c], hand[c], (((1,), (1,)), ((), ())), preferred_element_type=F32
             )
         outgoing[...] = packed.astype(BF16)
 
@@ -400,7 +424,7 @@
         device, there = a2a_target(i)
         return pltpu.make_async_remote_copy(
             outgoing.at[pl.ds(pl.multiple_of(there * 16, 16), 16)],
-            kown.at[pl.ds(pl.multiple_of(i * 16, 16), 16)],
+            kown.at[pl.ds(pl.multiple_of(i * 16 + (i // 16) * (OTHER - 256), 16), 16)],
             a2a_send.at[i],
             a2a_recv.at[i],
             device,
@@ -409,14 +433,42 @@
 
     def share_copy(i):
         return pltpu.make_async_remote_copy(
-            kown.at[pl.ds(i * 256, 256)],
-            kown.at[pl.ds(512 + i * 256, 256)],
+            kown.at[pl.ds(i * OTHER, 256)],
+            kown.at[pl.ds(i * OTHER + 256, 256)],
             share_send.at[i],
             share_recv.at[i],
             seq_peer,
             device_id_type=MESH,
         )
 
+    def own_part(lo, n):
+        part_scores = lax.dot_general(
+            qown[...],
+            kown[lo : lo + n, 0:EXT],
+            (((1,), (1,)), ((), ())),
+            preferred_element_type=F32,
+        )
+        column = lax.broadcasted_iota(jnp.int32, (1, 512), 1)
+        new_column = lax.broadcasted_iota(jnp.int32, (128, 128), 1)
+        new_step = lax.broadcasted_iota(jnp.int32, (128, 128), 0) // 32
+        for r in range(REQ):
+            rows = part_scores[r * 128 : (r + 1) * 128]
+            masked = jnp.where((column // 4) % 4 == r, rows[:, 0:512], masked_score)
+            if n > 512:
+                live = (new_column < 16) & (new_column % 4 == r) & (new_column // 4 <= new_step)
+                late = jnp.where(live, rows[:, 512:n], masked_score)
+                masked = jnp.concatenate([masked, late], axis=1)
+            masked = masked * score_scale
+            m_a = own_m[r]
+            top = jnp.maximum(m_a, jnp.max(masked, axis=1, keepdims=True))
+            e_a = jnp.exp2(m_a - top)
+            weights = jnp.exp2(masked - top[:, 0:1])
+            own_m[r] = top
+            own_l[r] = own_l[r] * e_a + jnp.sum(weights, axis=1, keepdims=True)
+            own_acc[r] = own_acc[r] * wide(e_a) + jnp.dot(
+                weights.astype(BF16), kown[lo : lo + n, 0:LATENT], preferred_element_type=F32
+            )
+
     def loop(lo, hi, f):
         def step(i, _):
             f(i)
@@ -425,16 +477,59 @@
         lax.fori_loop(lo, hi, step, 0)
 
     hooks = {
-        (1, 2): [lambda: rs_first(0)],
+        (0, 2): [before_handing],
+        (1, 0): [places],
+        (1, 1): [lambda: rs_first(0)],
         (2, 1): [lambda: rs_second(0)],
-        (2, 2): [lambda: seq_join(0)],
-        (2, 3): [lambda: rs_first(1)],
+        (2, 2): [lambda: rs_first(1), lambda: seq_join(0)],
         (3, 0): [lambda: rs_second(1)],
         (3, 1): [lambda: rs_first(2)],
-        (3, 2): [lambda: rs_second(2), lambda: rs_first(3), lambda: seq_join(1)],
-        (3, 3): [lambda: rs_second(3)],
+        (3, 2): [lambda: seq_join(1)],
+        (3, 3): [lambda: rs_second(2)],
+        (3, 4): [lambda: rs_first(3)],
+        (3, 6): [lambda: rs_second(3)],
+        (4, 1): [lambda: side_join(0)],
         (4, 2): [lambda: seq_join(2)],
     }
+
+    def phase(r, first, last):
+        step = KEYS // CHUNKS[r]
+
+        def chunk(c, _):
+            for (hook_r, hook_c), acts in hooks.items():
+                if hook_r == r:
+
+                    @pl.when(c == hook_c)
+                    def _():
+                        for act in acts:
+                            act()
+
+            at = pl.ds(pl.multiple_of(c * step, step), step)
+            if r < REQ:
+                fresh = jnp.dot(qx[r % 2], keys[r % 2, :, at], preferred_element_type=F32)
+                scores[r % 2, :, at] = fresh
+                top = tops[r % 2]
+                for j in range(step // 128):
+                    top = jnp.maximum(top, fresh[:, j * 128 : (j + 1) * 128])
+                tops[r % 2] = top
+            if r > 0:
+                b = r - 1
+                m = mstat[b]
+                ready = scores[b % 2, :, at]
+                weights = [
+                    jnp.exp2(ready[:, j * 128 : (j + 1) * 128] * score_scale - m)
+                    for j in range(step // 128)
+                ]
+                sums[...] += functools.reduce(jnp.add, weights)
+                acc[b] += lax.dot_general(
+                    jnp.concatenate(weights, axis=1).astype(BF16),
+                    keys[b % 2, 0:LATENT, at],
+                    (((1,), (1,)), ((), ())),
+                    preferred_element_type=F32,
+                )
+            return 0
+
+        lax.fori_loop(first, last, chunk, 0)
 
     for r in range(REQ + 1):
         if r < REQ:
@@ -449,86 +544,37 @@
             sums[...] = jnp.zeros((ROWS, 128), F32)
             acc[b] = jnp.zeros((ROWS, LATENT), F32)
 
-        def chunk(c, _):
-            for (hook_r, hook_c), acts in hooks.items():
-                if hook_r == r:
-
-                    @pl.when(c == hook_c)
-                    def _():
-                        for act in acts:
-                            act()
-
-            at = pl.ds(pl.multiple_of(c * CHUNK, CHUNK), CHUNK)
-            if r < REQ:
-                fresh = jnp.dot(qx[r % 2], keys[r % 2, :, at], preferred_element_type=F32)
-                scores[r % 2, :, at] = fresh
-                top = tops[r % 2]
-                for j in range(CHUNK // 128):
-                    top = jnp.maximum(top, fresh[:, j * 128 : (j + 1) * 128])
-                tops[r % 2] = top
-            if r > 0:
-                b = r - 1
-                m = mstat[b]
-                ready = scores[b % 2, :, at]
-                weights = [
-                    jnp.exp2(ready[:, j * 128 : (j + 1) * 128] * score_scale - m)
-                    for j in range(CHUNK // 128)
-                ]
-                sums[...] += functools.reduce(jnp.add, weights)
-                acc[b] += lax.dot_general(
-                    jnp.concatenate(weights, axis=1).astype(BF16),
-                    keys[b % 2, 0:LATENT, at],
-                    (((1,), (1,)), ((), ())),
-                    preferred_element_type=F32,
-                )
-            return 0
-
-        lax.fori_loop(0, CHUNKS, chunk, 0)
-        if r > 0:
+        phase(r, 0, CHUNKS[r] if r < REQ else CUTS[0])
+        if 0 < r < REQ:
             seq_start(r - 1)
             if r + 1 < REQ:
                 key_copy(r + 1).start()
 
     handed()
     hand_copy.start()
-    seq_join(3)
-    side_join(0)
-    id_copy.wait_recv()
+    phase(REQ, CUTS[0], CUTS[1])
     hand_copy.wait_recv()
+    pl.semaphore_signal(ready, inc=1, device_id=side_peer, device_id_type=MESH)
     pack_rows()
-    loop(0, 32, lambda i: a2a_copy(i).start())
+    loop(0, 16, lambda i: a2a_copy(i).start())
+    pl.semaphore_wait(ready, 1)
+    loop(16, 32, lambda i: a2a_copy(i).start())
+    phase(REQ, CUTS[1], CHUNKS[REQ])
+    seq_start(3)
     side_join(1)
     side_join(2)
-    side_join(3)
     loop(0, 16, lambda i: a2a_copy(i).wait_recv())
     share_copy(0).start()
+    seq_join(3)
+    share_copy(0).wait_recv()
+    own_part(0, OTHER)
     loop(16, 32, lambda i: a2a_copy(i).wait_recv())
     share_copy(1).start()
-    share_copy(0).wait_recv()
+    side_join(3)
     share_copy(1).wait_recv()
-
-    own_scores = lax.dot_general(
-        qown[...], kown[:, 0:EXT], (((1,), (1,)), ((), ())), preferred_element_type=F32
-    )
-    column = lax.broadcasted_iota(jnp.int32, (1, 1024), 1)
-    new_column = lax.broadcasted_iota(jnp.int32, (128, 128), 1)
-    new_step = lax.broadcasted_iota(jnp.int32, (128, 128), 0) // 32
+    own_part(OTHER, 512)
     for r in range(REQ):
-        rows = own_scores[r * 128 : (r + 1) * 128]
-        old = jnp.where((column // 4) % 4 == r, rows[:, 0:1024], masked_score)
-        live = (new_column < 16) & (new_column % 4 == r) & (new_column // 4 <= new_step)
-        late = jnp.where(live, rows[:, 1024:1152], masked_score)
-        everything = jnp.concatenate([old, late], axis=1) * score_scale
-        m_b = jnp.max(everything, axis=1, keepdims=True)
-        weights = jnp.exp2(everything - m_b)
-        l_b = jnp.sum(weights, axis=1, keepdims=True)
-        acc_b = jnp.dot(weights.astype(BF16), kown[:, 0:LATENT], preferred_element_type=F32)
-        m_a = own_m[r][:, 0:1]
-        l_a = own_l[r][:, 0:1]
-        top = jnp.maximum(m_a, m_b)
-        e_a, e_b = jnp.exp2(m_a - top), jnp.exp2(m_b - top)
-        total = l_a * e_a + l_b * e_b
-        result = (own_acc[r] * e_a + acc_b * e_b) / total
+        result = own_acc[r] / wide(own_l[r])
         for s in range(4):
             out_ref[s, r] = result[s * 32 : (s + 1) * 32].astype(BF16)
 
@@ -583,9 +629,10 @@
             pltpu.VMEM((REQ, ROWS, LATENT), F32),
             pltpu.VMEM((REQ, ROWS, 128), F32),
             pltpu.VMEM((REQ, ROWS, 128), F32),
-            pltpu.VMEM((REQ, 256, LATENT), F32),
-            pltpu.VMEM((REQ, 256, 128), F32),
-            pltpu.VMEM((REQ, 256, 128), F32),
+            pltpu.VMEM((REQ, 2, 128, LATENT), BF16),
+            pltpu.VMEM((REQ, 2, 128, LATENT), BF16),
+            pltpu.VMEM((REQ, 2, 8, 128), F32),
+            pltpu.VMEM((REQ, 2, 8, 128), F32),
             pltpu.VMEM((REQ, 128, LATENT), BF16),
             pltpu.VMEM((REQ, 128, LATENT), BF16),
             pltpu.VMEM((REQ, 8, 128), F32),
@@ -597,12 +644,15 @@
             pltpu.VMEM((2, PAD, 128), BF16),
             pltpu.VMEM((256, PAD), BF16),
             pltpu.VMEM((1152, PAD), BF16),
+            pltpu.VMEM((LATENT, 128), F32),
+            pltpu.VMEM((2, 32, 128), F32),
+            pltpu.VMEM((2, 256, 128), BF16),
             dma((3,)),
             dma((2,)),
             dma((36,)),
             dma((36,)),
-            dma((12,)),
-            dma((12,)),
+            dma((8,)),
+            dma((8,)),
             dma((8,)),
             dma((8,)),
             dma((2,)),
@@ -611,6 +661,7 @@
             dma((32,)),
             dma((2,)),
             dma((2,)),
+            pltpu.SemaphoreType.REGULAR,
         ],
         compiler_params=pltpu.CompilerParams(
             collective_id=0, has_side_effects=True, vmem_limit_bytes=62 << 20

time: 73.8 us -> 68.5 us (0.928)
  Pallas kernels: 71.6 us -> 66.2 us
    pallas_call x1, Pallas kernels: 71.6 us -> 66.2 us  [on_device(): pl.pallas_call(kernel, out_shape=jax.ShapeDtypeStruct((4, 4, 32, LATENT),...]
where the time goes in v2:
time: 68.5 us; the launch traced here: 68.1 us
  Pallas kernels  66.2 us (97%)
  local copies, waits for them, and re-layouts  1.88 us (3%)
    pallas_call x1, Pallas kernels, on_device(): pl.pallas_call(kernel, out_shape=jax.ShapeDtypeStruct((4, 4, 32, LATENT),...  66.2 us
    unnamed x1, local copies, waits for them, and re-layouts  1.88 us

profile of v2, /device:TPU:1, one launch (start us, length us, event | category | flops | bytes accessed | tf_op | source)
XLA Modules:
  0.0 68.1 jit_solution(5545271167709839161)
XLA Ops:
  0.0 66.2 %shard_map.100 = bf16[4,4,32,512]{3,2,1,0:T(8,128)(2,1)} custom-call(s32[4]{0:T(128)} %lens_ref.1, s32[4]{0:T(128)} %plens_ref.1, bf16[224,4096]{1,0:T(8,128)(2,1)} %bitcast.8, bf16[224,576]{1,0:T(8,128)(2,1)} %w_hbm.1, f32[1,512]{1,0:T(1,128)} %bitcast.10, s32[1,4096]{1,0:T(1,128)} %bitcast.9, s32[1,128]{1,0:T(1,128)} %bitcast.11, ...), custom_call_target="tpu_custom_call" | custom-call | flops 20000000000 | bytes 24000000 | tf_op jit(solution)/shard_map/pallas_call | solution.py:611
  66.3 1.9 %copy.12 = bf16[4,4,32,512]{3,2,1,0:T(8,128)(2,1)} copy(bf16[4,4,32,512]{3,2,1,0:T(8,128)(2,1)} %shard_map.100) | data formatting | bytes 1048576

commit v3 on v2

--- a/solution.py
+++ b/solution.py
@@ -18,23 +18,26 @@
 PAD = 640
 HEADS = 128
 KEYS = 4096
-CHUNKS = (4, 4, 4, 8, 8)
-CUTS = (4, 6)
+CHUNKS = (4, 4, 4, 4)
+CUTS = (3, 3)
 REQ = 4
 ROWS = 512
 PIECE = WIDTH // 4
 NEW = 512
 OTHER = NEW + 128
+EARLY_Y = 3
 RING_MASKS = (2, 8, 6, 24)
 F32 = jnp.float32
 BF16 = jnp.bfloat16
 
 
-def piece_slot(piece, flips):
+def piece_slot(piece, flips, y_flip):
     slot = 0
     for i in range(4):
+        if i == 3 and piece == EARLY_Y:
+            slot = slot * 2 + y_flip
         slot = slot * 2 + ((flips >> ((piece + i) % 4)) & 1)
-    return slot
+    return slot if piece == EARLY_Y else slot * 2 + y_flip
 
 
 def flips_mask(flips):
@@ -181,7 +184,7 @@
         for half in range(2):
             rel = (half + y) % 2
             for p in range(4):
-                part[p, piece_slot(p, flips) * 2 + rel] = block[
+                part[p, piece_slot(p, flips, rel)] = block[
                     p * PIECE : (p + 1) * PIECE, half * 128 : (half + 1) * 128
                 ]
 
@@ -191,11 +194,11 @@
         held = 32 >> stage
         if stage == 4:
             lo, n = 1, 1
-            peer = rs_peers[4]
+            peer = rs_peers[(p + 3) % 4 if p == EARLY_Y else 4]
         else:
             n = held // 4
             lo = held // 2 + (n if sub_part == 0 else 0)
-            peer = rs_peers[(p + stage) % 4]
+            peer = rs_peers[4 if stage == 3 and p == EARLY_Y else (p + stage) % 4]
         index = (stage * 2 + sub_part) * 4 + p
         return pltpu.make_async_remote_copy(
             part.at[p, pl.ds(lo, n)],
@@ -210,30 +213,27 @@
         for p in range(4):
             rs_copy(stage, p, sub_part).start()
 
-    def rs_start(stage):
-        rs_part(stage, 0)
-        if stage < 4:
-            rs_part(stage, 1)
-
-    def rs_take(stage, sub_part):
+    def rs_take(stage, sub_part, p):
         held = 32 >> stage
         n = held // 4
         lo = n if sub_part == 0 else 0
+        rs_copy(stage, p, sub_part).wait_recv()
+
+        def add(j, _):
+            part[p, lo + j] = part[p, lo + j] + landed[p, starts[stage] + lo + j]
+            return 0
+
+        lax.fori_loop(0, n, add, 0)
+
+    def rs_first(stage):
         for p in range(4):
-            rs_copy(stage, p, sub_part).wait_recv()
-
-            def add(j, _):
-                part[p, lo + j] = part[p, lo + j] + landed[p, starts[stage] + lo + j]
-                return 0
-
-            lax.fori_loop(0, n, add, 0)
-
-    def rs_first(stage):
-        rs_take(stage, 0)
-        rs_start(stage + 1)
+            rs_take(stage, 0, p)
+            for sub_part in range(2 if stage < 3 else 1):
+                rs_copy(stage + 1, p, sub_part).start()
 
     def rs_second(stage):
-        rs_take(stage, 1)
+        for p in range(4):
+            rs_take(stage, 1, p)
 
     for flips in (15, 7, 11, 13, 14, 3, 6, 12, 9):
         project(flips)
@@ -478,90 +478,83 @@
 
     hooks = {
         (0, 2): [before_handing],
-        (1, 0): [places],
-        (1, 1): [lambda: rs_first(0)],
-        (2, 1): [lambda: rs_second(0)],
-        (2, 2): [lambda: rs_first(1), lambda: seq_join(0)],
-        (3, 0): [lambda: rs_second(1)],
-        (3, 1): [lambda: rs_first(2)],
-        (3, 2): [lambda: seq_join(1)],
-        (3, 3): [lambda: rs_second(2)],
-        (3, 4): [lambda: rs_first(3)],
-        (3, 6): [lambda: rs_second(3)],
-        (4, 1): [lambda: side_join(0)],
-        (4, 2): [lambda: seq_join(2)],
+        (0, 3): [places],
+        (1, 0): [lambda: rs_first(0)],
+        (1, 3): [lambda: rs_second(0), lambda: seq_join(0)],
+        (2, 0): [lambda: rs_first(1)],
+        (2, 1): [lambda: side_join(0)],
+        (2, 2): [lambda: rs_second(1)],
+        (2, 3): [lambda: rs_first(2), lambda: seq_join(1)],
+        (3, 0): [lambda: rs_second(2)],
+        (3, 1): [lambda: rs_first(3)],
+        (3, 2): [lambda: rs_second(3), lambda: seq_join(2), lambda: side_join(1)],
     }
 
-    def phase(r, first, last):
+    def fresh_scores(r, c):
         step = KEYS // CHUNKS[r]
-
-        def chunk(c, _):
-            for (hook_r, hook_c), acts in hooks.items():
-                if hook_r == r:
-
-                    @pl.when(c == hook_c)
-                    def _():
-                        for act in acts:
-                            act()
-
-            at = pl.ds(pl.multiple_of(c * step, step), step)
-            if r < REQ:
-                fresh = jnp.dot(qx[r % 2], keys[r % 2, :, at], preferred_element_type=F32)
-                scores[r % 2, :, at] = fresh
-                top = tops[r % 2]
-                for j in range(step // 128):
-                    top = jnp.maximum(top, fresh[:, j * 128 : (j + 1) * 128])
-                tops[r % 2] = top
-            if r > 0:
-                b = r - 1
-                m = mstat[b]
-                ready = scores[b % 2, :, at]
-                weights = [
-                    jnp.exp2(ready[:, j * 128 : (j + 1) * 128] * score_scale - m)
-                    for j in range(step // 128)
-                ]
-                sums[...] += functools.reduce(jnp.add, weights)
-                acc[b] += lax.dot_general(
-                    jnp.concatenate(weights, axis=1).astype(BF16),
-                    keys[b % 2, 0:LATENT, at],
-                    (((1,), (1,)), ((), ())),
-                    preferred_element_type=F32,
-                )
-            return 0
-
-        lax.fori_loop(first, last, chunk, 0)
-
-    for r in range(REQ + 1):
-        if r < REQ:
-            queries_in(r)
-            dead_row(r)
-            tops[r % 2] = jnp.full((ROWS, 128), -3e38, F32)
-            key_copy(r).wait()
+        at = pl.ds(c * step, step)
+        fresh = jnp.dot(qx[r % 2], keys[r % 2, :, at], preferred_element_type=F32)
+        scores[c % 2, :, 0:step] = fresh
+        tops[c % 2] = functools.reduce(
+            jnp.maximum, [fresh[:, j * 128 : (j + 1) * 128] for j in range(step // 128)]
+        )
+
+    def weigh(r, c):
+        step = KEYS // CHUNKS[r]
+        at = pl.ds(c * step, step)
+        before = mstat[r]
+        m = jnp.maximum(before, jnp.max(tops[c % 2], axis=1, keepdims=True) * score_scale)
+        mstat[r] = m
+        fade = jnp.exp2(before - m)
+        ready = scores[c % 2, :, 0:step]
+        weights = [
+            jnp.exp2(ready[:, j * 128 : (j + 1) * 128] * score_scale - m)
+            for j in range(step // 128)
+        ]
+        sums[...] = sums[...] * fade + functools.reduce(jnp.add, weights)
+        acc[r] = acc[r] * wide(fade) + lax.dot_general(
+            jnp.concatenate(weights, axis=1).astype(BF16),
+            keys[r % 2, 0:LATENT, at],
+            (((1,), (1,)), ((), ())),
+            preferred_element_type=F32,
+        )
+
+    def chunks(r, first, last):
+        for c in range(first, last):
+            for act in hooks.get((r, c), ()):
+                act()
+            fresh_scores(r, c)
+            weigh(r, c - 1)
+
+    for r in range(REQ):
+        queries_in(r)
+        dead_row(r)
+        key_copy(r).wait()
+        for act in hooks.get((r, 0), ()):
+            act()
+        fresh_scores(r, 0)
         if r > 0:
-            b = r - 1
-            top = jnp.max(tops[b % 2], axis=1, keepdims=True) * score_scale
-            mstat[b] = jnp.broadcast_to(top, (ROWS, 128))
-            sums[...] = jnp.zeros((ROWS, 128), F32)
-            acc[b] = jnp.zeros((ROWS, LATENT), F32)
-
-        phase(r, 0, CHUNKS[r] if r < REQ else CUTS[0])
-        if 0 < r < REQ:
+            weigh(r - 1, CHUNKS[r - 1] - 1)
             seq_start(r - 1)
             if r + 1 < REQ:
                 key_copy(r + 1).start()
+        mstat[r] = jnp.full((ROWS, 128), -3e38, F32)
+        sums[...] = jnp.zeros((ROWS, 128), F32)
+        acc[r] = jnp.zeros((ROWS, LATENT), F32)
+        chunks(r, 1, CHUNKS[r] if r + 1 < REQ else CUTS[0])
 
     handed()
     hand_copy.start()
-    phase(REQ, CUTS[0], CUTS[1])
+    chunks(REQ - 1, CUTS[0], CUTS[1])
     hand_copy.wait_recv()
     pl.semaphore_signal(ready, inc=1, device_id=side_peer, device_id_type=MESH)
     pack_rows()
     loop(0, 16, lambda i: a2a_copy(i).start())
     pl.semaphore_wait(ready, 1)
     loop(16, 32, lambda i: a2a_copy(i).start())
-    phase(REQ, CUTS[1], CHUNKS[REQ])
+    chunks(REQ - 1, CUTS[1], CHUNKS[REQ - 1])
+    weigh(REQ - 1, CHUNKS[REQ - 1] - 1)
     seq_start(3)
-    side_join(1)
     side_join(2)
     loop(0, 16, lambda i: a2a_copy(i).wait_recv())
     share_copy(0).start()
@@ -623,7 +616,7 @@
             pltpu.VMEM((4, 4, WIDTH, HEADS), BF16),
             pltpu.VMEM((2, ROWS, EXT), BF16),
             pltpu.VMEM((ROWS, EXT), BF16),
-            pltpu.VMEM((2, ROWS, KEYS), F32),
+            pltpu.VMEM((2, ROWS, KEYS // 4), F32),
             pltpu.VMEM((2, ROWS, 128), F32),
             pltpu.VMEM((ROWS, 128), F32),
             pltpu.VMEM((REQ, ROWS, LATENT), F32),

time: 68.5 us -> 62.9 us (0.918); the launches traced: 68.1 us -> 61.8 us
  Pallas kernels: 66.2 us -> 60 us
    pallas_call x1, Pallas kernels: 66.2 us -> 60 us  [on_device(): pl.pallas_call(kernel, out_shape=jax.ShapeDtypeStruct((4, 4, 32, LATENT),...]
where the time goes in v3:
time: 62.9 us; the launch traced here: 61.8 us
  Pallas kernels  60 us (95%)
  local copies, waits for them, and re-layouts  1.88 us (3%)
    pallas_call x1, Pallas kernels, on_device(): pl.pallas_call(kernel, out_shape=jax.ShapeDtypeStruct((4, 4, 32, LATENT),...  60 us
    unnamed x1, local copies, waits for them, and re-layouts  1.88 us

profile of v3, /device:TPU:1, one launch (start us, length us, event | category | flops | bytes accessed | tf_op | source)
XLA Modules:
  0.0 61.8 jit_solution(4667763572409796541)
XLA Ops:
  0.0 60.0 %shard_map.100 = bf16[4,4,32,512]{3,2,1,0:T(8,128)(2,1)} custom-call(s32[4]{0:T(128)} %lens_ref.1, s32[4]{0:T(128)} %plens_ref.1, bf16[224,4096]{1,0:T(8,128)(2,1)} %bitcast.8, bf16[224,576]{1,0:T(8,128)(2,1)} %w_hbm.1, f32[1,512]{1,0:T(1,128)} %bitcast.10, s32[1,4096]{1,0:T(1,128)} %bitcast.9, s32[1,128]{1,0:T(1,128)} %bitcast.11, ...), custom_call_target="tpu_custom_call" | custom-call | flops 20000000000 | bytes 24000000 | tf_op jit(solution)/shard_map/pallas_call | solution.py:604
  60.0 1.9 %copy.12 = bf16[4,4,32,512]{3,2,1,0:T(8,128)(2,1)} copy(bf16[4,4,32,512]{3,2,1,0:T(8,128)(2,1)} %shard_map.100) | data formatting | bytes 1048576
